TPU v7x, 256 devices: a whole 4x4x8 slice. The times are simulated.
256 devices in a mesh: outer: 32 (over z, y_hi, core), inner: 8 (over x, y_lo).
Axes of the slice: x: 4, y: 4 (y_hi: 2, y_lo: 2; y = y_hi * 2 + y_lo), z: 8, core: 2. Of those that a mesh axis runs over, the one named last changes fastest.
Arguments:
- image_emb: bfloat16 [131072, 1152], P(('outer', 'inner'))
- text_emb: bfloat16 [131072, 1152], P(('outer', 'inner'))
- positive: int32 [131072], P(('outer', 'inner')), may hold values from 0 to 131071, as said below
- log_temp: float32 [1], replicated, may hold values from 1 to 2
- bias: float32 [1], replicated, may hold values from -3 to -1
Outputs:
- loss: float32 [1], replicated
- grad_image: float32 [131072, 1152], P(('outer', 'inner'))
- grad_text: float32 [131072, 1152], P(('outer', 'inner'))
Inputs may be any that keep to these rules, and one draw needn't show every extreme that they name: positive maps each aligned block of 512 rows one to one onto the text indices of the same block.
All inputs are finite; a program needn't handle non-finite values.
Results may differ from a plain program's by a relative error of at most 0.00033.
Values may be sent and summed in bfloat16 or wider, within the bound.
A program may use at most 64 MiB of HBM per device.

v0:
```python
import jax
import jax.numpy as jnp
from jax import lax
from jax.sharding import PartitionSpec as P

HOPS = ((0, 0), (0, 1), (0, 2), (0, 3), (1, 3))


def from_behind(value, axis, steps):
    count = lax.axis_size(axis)
    pairs = [(source, (source + steps) % count) for source in range(count)]
    return lax.ppermute(value, axis, pairs)


def normalize(x):
    xf = x.astype(jnp.float32)
    inv = lax.rsqrt(jnp.sum(xf * xf, axis=1, keepdims=True) + 1e-06)
    return (xf * inv, inv)


def tile_coef(z_img, z_txt, text_block, pos_rows, temp, shift_b):
    rows = z_txt.shape[0]
    scores = jnp.einsum("bd,cd->bc", z_img, z_txt, preferred_element_type=jnp.float32)
    logit = temp * scores + shift_b
    columns = text_block * rows + jnp.arange(rows, dtype=jnp.int32)
    label = (pos_rows[:, None] == columns[None, :]).astype(jnp.float32)
    term = jnp.sum(jax.nn.softplus(-(2.0 * label - 1.0) * logit))
    coef = (jax.nn.sigmoid(logit) - label).astype(jnp.bfloat16)
    return (term, coef)


def text_terms(coef, z_img):
    return jnp.einsum("bc,bd->cd", coef, z_img, preferred_element_type=jnp.float32)


def move_text(block, hop_prev, hop_next):
    if hop_next[0] != hop_prev[0]:
        return from_behind(block, "outer", 1)
    return from_behind(block, "inner", 1)


def move_sums(sums, hop_prev, hop_next):
    if hop_next[0] != hop_prev[0]:
        return from_behind(sums, "outer", 1)
    return from_behind(sums, "inner", 1)


def body(image_emb, text_emb, positive, log_temp, bias):
    temp = jnp.exp(log_temp[0])
    shift_b = bias[0]
    n_outer = lax.axis_size("outer")
    n_inner = lax.axis_size("inner")
    where_outer = lax.axis_index("outer")
    where_inner = lax.axis_index("inner")
    zn_img, inv_img = normalize(image_emb)
    zn_txt, inv_txt = normalize(text_emb)
    z_img = zn_img.astype(jnp.bfloat16)
    z_txt = zn_txt.astype(jnp.bfloat16)
    held = z_txt
    d_image = jnp.zeros(zn_img.shape, jnp.float32)
    total = jnp.zeros((), jnp.float32)
    carried = jnp.zeros(zn_txt.shape, jnp.float32)
    for step, hop in enumerate(HOPS):
        if step > 0:
            held = move_text(held, HOPS[step - 1], hop)
            carried = move_sums(carried, HOPS[step - 1], hop)
        text_block = (where_outer - hop[0]) % n_outer * n_inner + (where_inner - hop[1]) % n_inner
        term, coef = tile_coef(z_img, held, text_block, positive, temp, shift_b)
        total = total + term
        d_image = d_image + jnp.dot(coef, held, preferred_element_type=jnp.float32)
        carried = carried + text_terms(coef, z_img)
    back = from_behind(carried, "outer", -1)
    d_text = from_behind(back, "inner", -3)
    total = lax.psum(total, ("outer", "inner"))
    d_image = temp * d_image
    d_text = temp * d_text
    grad_image = (d_image - zn_img * jnp.sum(zn_img * d_image, axis=1, keepdims=True)) * inv_img
    grad_text = (d_text - zn_txt * jnp.sum(zn_txt * d_text, axis=1, keepdims=True)) * inv_txt
    count = image_emb.shape[0] * n_outer * n_inner
    loss = jnp.reshape(total / count, (1,))
    return (loss, grad_image, grad_text)


def solution(mesh):
    placed = (
        P(("outer", "inner"), None),
        P(("outer", "inner"), None),
        P(("outer", "inner")),
        P(),
        P(),
    )
    return jax.shard_map(
        body,
        mesh=mesh,
        in_specs=placed,
        out_specs=(P(), P(("outer", "inner"), None), P(("outer", "inner"), None)),
        check_vma=False,
    )
```

profile of v0, /device:TPU:1, one launch (start us, length us, event | category | flops | bytes accessed | tf_op | source)
XLA Modules:
  0.0 466.2 jit_solution(3615324479071295987)
XLA Ops:
  0.7 1.7 fusion.14
  2.3 1.5 fusion.3
  6.5 2.4 fusion.61
  8.9 2.1 collective-permute-start.4
  11.1 1.1 collective-permute-start
  12.2 75.5 %collective-permute-done = bf16[512,1152]{1,0:T(8,128)(2,1)} collective-permute-done((bf16[512,1152]{1,0:T(8,128)(2,1)S(1)}, bf16[512,1152]{1,0:T(8,128)(2,1)}, u32[]{:S(2)}, u32[]{:S(2)}) %collective-permute-start) | collective-permute-done | bytes 1179680 | tf_op jit(solution)/shard_map/ppermute | solution.py:12
  87.7 2.2 fusion.18
  89.8 3.1 convolution_add_fusion
  94.0 2.2 collective-permute-start.1
  96.2 73.7 %collective-permute-done.1 = bf16[512,1152]{1,0:T(8,128)(2,1)} collective-permute-done((bf16[512,1152]{1,0:T(8,128)(2,1)}, bf16[512,1152]{1,0:T(8,128)(2,1)}, u32[]{:S(2)}, u32[]{:S(2)}) %collective-permute-start.1) | collective-permute-done | bytes 1179680 | tf_op jit(solution)/shard_map/ppermute | solution.py:12
  169.8 2.2 fusion.17
  172.0 1.7 fusion.56
  173.8 1.9 add.252
  176.4 3.1 collective-permute-start.2
  179.5 72.1 %collective-permute-done.2 = bf16[512,1152]{1,0:T(8,128)(2,1)} collective-permute-done((bf16[512,1152]{1,0:T(8,128)(2,1)}, bf16[512,1152]{1,0:T(8,128)(2,1)}, u32[]{:S(2)}, u32[]{:S(2)}) %collective-permute-start.2) | collective-permute-done | bytes 1179680 | tf_op jit(solution)/shard_map/ppermute | solution.py:12
  251.7 11.8 %collective-permute-start.3 = (bf16[512,1152]{1,0:T(8,128)(2,1)}, bf16[512,1152]{1,0:T(8,128)(2,1)}, u32[]{:S(2)}, u32[]{:S(2)}) collective-permute-start(bf16[512,1152]{1,0:T(8,128)(2,1)} %collective-permute-done.2), channel_id=1, source_target_pairs={{0,8},{8,16},{16,24},{24,32},{32,40},{40,48},{48,56},{56,64},{64,7... | collective-permute-start | bytes 3538952 | tf_op jit(solution)/shard_map/ppermute | solution.py:12
  263.5 2.2 fusion.16
  265.7 1.7 fusion.53
  267.4 1.9 add.253
  269.5 7.5 %collective-permute-done.3 = bf16[512,1152]{1,0:T(8,128)(2,1)} collective-permute-done((bf16[512,1152]{1,0:T(8,128)(2,1)}, bf16[512,1152]{1,0:T(8,128)(2,1)}, u32[]{:S(2)}, u32[]{:S(2)}) %collective-permute-start.3) | collective-permute-done | bytes 1179680 | tf_op jit(solution)/shard_map/ppermute | solution.py:12
  277.0 7.4 %fusion.49 = (f32[]{:T(128)}, f32[]{:T(128)}, f32[]{:T(128)}, f32[]{:T(128)}, f32[]{:T(128)}, /*index=5*/f32[512,512]{1,0:T(8,128)S(1)}) fusion(s32[512]{0:T(512)S(1)} %iota_add_fusion, s32[512]{0:T(512)} %param.7, f32[512,512]{1,0:T(8,128)} %copy-done.12, s32[512]{0:T(512)S(1)} %iota_add_fusion.3, f32[512,512]{1,0:T(8,128)} %copy-done.14, ...), kind=kOutput, calls=%fused_computation.78 | convolution fusion | flops 622002176 | bytes 7616540 | tf_op jit(solution)/shard_map/bd,cd->bc/dot_general | solution.py:23
  285.5 16.7 %collective-permute-done.7 = f32[512,1152]{1,0:T(8,128)} collective-permute-done((f32[512,1152]{1,0:T(8,128)S(1)}, f32[512,1152]{1,0:T(8,128)}, u32[]{:S(2)}, u32[]{:S(2)}) %collective-permute-start.7) | collective-permute-done | bytes 2359328 | tf_op jit(solution)/shard_map/ppermute | solution.py:12
  302.1 1.9 add.254
  304.0 3.4 collective-permute-start.8
  308.4 26.4 %collective-permute-done.8 = f32[512,1152]{1,0:T(8,128)} collective-permute-done((f32[512,1152]{1,0:T(8,128)S(1)}, f32[512,1152]{1,0:T(8,128)}, u32[]{:S(2)}, u32[]{:S(2)}) %collective-permute-start.8) | collective-permute-done | bytes 2359328 | tf_op jit(solution)/shard_map/ppermute | solution.py:12
  334.8 2.3 convolution_add_fusion.4
  337.2 3.7 convolution_add_fusion.3
  344.2 4.8 %convolution_add_fusion.2 = f32[512,1152]{1,0:T(8,128)} fusion(f32[512,1152]{1,0:T(8,128)} %convolution_add_fusion.3, bf16[512,1152]{1,0:T(8,128)(2,1)} %collective-permute-done.2, f32[512,512]{1,0:T(8,128)} %copy-done.16, s32[512]{0:T(512)S(1)} %copy-done.7, s32[512]{0:T(512)} %param.7), kind=kOutput, calls=%fused_computation.2 | convolution fusion | flops 606404608 | bytes 6950912 | tf_op jit(solution)/shard_map/dot_general | solution.py:70
  349.0 107.5 %psum.7 = f32[]{:T(128)} all-reduce(f32[]{:T(128)S(6)} %add.241), channel_id=1, replica_groups=mesh['outer'=32,'inner'=8] {'outer','inner'}, use_global_device_ids=true, to_apply=%region_7.8 | all-reduce | flops 1 | bytes 8 | tf_op jit(solution)/shard_map/psum | solution.py:74
  457.2 3.5 fusion.7
  460.7 1.9 fusion.9
  463.1 2.0 fusion.13
  (60 shorter events, 5.8 us)
Async XLA Ops:
  0.6 4.6 copy-start.1
  3.9 7.2 %copy-start.2 = (bf16[512,1152]{1,0:T(8,128)(2,1)}, bf16[512,1152]{1,0:T(8,128)(2,1)S(1)}, u32[]{:S(2)}) copy-start(bf16[512,1152]{1,0:T(8,128)(2,1)S(1)} %fusion.3) | copy-start | bytes 3538948
  5.5 1.0 copy-start.10
  6.5 2.4 copy-start.17
  8.9 80.9 %collective-permute-start.4 = (f32[512,1152]{1,0:T(8,128)}, f32[512,1152]{1,0:T(8,128)}, u32[]{:S(2)}, u32[]{:S(2)}) collective-permute-start(f32[512,1152]{1,0:T(8,128)} %fusion.61), channel_id=1, source_target_pairs={{0,1},{1,2},{2,3},{3,4},{4,5},{5,6},{6,7},{7,0},{8,9},{9,10},{10,1... | collective-permute-start | bytes 7077896 | tf_op jit(solution)/shard_map/ppermute | solution.py:12
  11.1 76.6 %collective-permute-start = (bf16[512,1152]{1,0:T(8,128)(2,1)S(1)}, bf16[512,1152]{1,0:T(8,128)(2,1)}, u32[]{:S(2)}, u32[]{:S(2)}) collective-permute-start(bf16[512,1152]{1,0:T(8,128)(2,1)S(1)} %fusion.3), channel_id=1, source_target_pairs={{0,1},{1,2},{2,3},{3,4},{4,5},{5,6},{6,7},{7,0},{8,9},{9,10},{10,1... | collective-permute-start | bytes 3538952 | tf_op jit(solution)/shard_map/ppermute | solution.py:12
  89.8 3.1 copy-start.12
  92.9 80.8 %collective-permute-start.5 = (f32[512,1152]{1,0:T(8,128)S(1)}, f32[512,1152]{1,0:T(8,128)}, u32[]{:S(2)}, u32[]{:S(2)}) collective-permute-start(f32[512,1152]{1,0:T(8,128)S(1)} %convolution_add_fusion), channel_id=1, source_target_pairs={{0,1},{1,2},{2,3},{3,4},{4,5},{5,6},{6,7},{7,0},{8,9},{9,10},{10,1... | collective-permute-start | bytes 7077896 | tf_op jit(solution)/shard_map/ppermute | solution.py:12
  94.0 75.9 %collective-permute-start.1 = (bf16[512,1152]{1,0:T(8,128)(2,1)}, bf16[512,1152]{1,0:T(8,128)(2,1)}, u32[]{:S(2)}, u32[]{:S(2)}) collective-permute-start(bf16[512,1152]{1,0:T(8,128)(2,1)} %collective-permute-done), channel_id=1, source_target_pairs={{0,1},{1,2},{2,3},{3,4},{4,5},{5,6},{6,7},{7,0},{8,9},{9,10},{10,1... | collective-permute-start | bytes 3538952 | tf_op jit(solution)/shard_map/ppermute | solution.py:12
  96.2 77.6 %copy-start.4 = (s32[512]{0:T(512)}, s32[512]{0:T(512)S(1)}, u32[]{:S(2)}) copy-start(s32[512]{0:T(512)S(1)} %iota_add_fusion.2) | copy-start | bytes 6148
  172.0 1.8 copy-start.14
  175.7 91.8 %collective-permute-start.6 = (f32[512,1152]{1,0:T(8,128)S(1)}, f32[512,1152]{1,0:T(8,128)}, u32[]{:S(2)}, u32[]{:S(2)}) collective-permute-start(f32[512,1152]{1,0:T(8,128)S(1)} %add.252), channel_id=1, source_target_pairs={{0,1},{1,2},{2,3},{3,4},{4,5},{5,6},{6,7},{7,0},{8,9},{9,10},{10,1... | collective-permute-start | bytes 7077896 | tf_op jit(solution)/shard_map/ppermute | solution.py:12
  176.4 75.2 %collective-permute-start.2 = (bf16[512,1152]{1,0:T(8,128)(2,1)}, bf16[512,1152]{1,0:T(8,128)(2,1)}, u32[]{:S(2)}, u32[]{:S(2)}) collective-permute-start(bf16[512,1152]{1,0:T(8,128)(2,1)} %collective-permute-done.1), channel_id=1, source_target_pairs={{0,1},{1,2},{2,3},{3,4},{4,5},{5,6},{6,7},{7,0},{8,9},{9,10},{10,1... | collective-permute-start | bytes 3538952 | tf_op jit(solution)/shard_map/ppermute | solution.py:12
  179.5 87.9 %copy-start.6 = (s32[512]{0:T(512)}, s32[512]{0:T(512)S(1)}, u32[]{:S(2)}) copy-start(s32[512]{0:T(512)S(1)} %iota_add_fusion.1) | copy-start | bytes 6148
  251.7 25.3 %collective-permute-start.3 = (bf16[512,1152]{1,0:T(8,128)(2,1)}, bf16[512,1152]{1,0:T(8,128)(2,1)}, u32[]{:S(2)}, u32[]{:S(2)}) collective-permute-start(bf16[512,1152]{1,0:T(8,128)(2,1)} %collective-permute-done.2), channel_id=1, source_target_pairs={{0,8},{8,16},{16,24},{24,32},{32,40},{40,48},{48,56},{56,64},{64,7... | collective-permute-start | bytes 3538952 | tf_op jit(solution)/shard_map/ppermute | solution.py:12
  265.7 1.8 copy-start.16
  269.3 32.8 %collective-permute-start.7 = (f32[512,1152]{1,0:T(8,128)S(1)}, f32[512,1152]{1,0:T(8,128)}, u32[]{:S(2)}, u32[]{:S(2)}) collective-permute-start(f32[512,1152]{1,0:T(8,128)S(1)} %add.253), channel_id=1, source_target_pairs={{0,8},{8,16},{16,24},{24,32},{32,40},{40,48},{48,56},{56,64},{64,7... | collective-permute-start | bytes 7077896 | tf_op jit(solution)/shard_map/ppermute | solution.py:12
  269.5 14.9 %copy-start.8 = (s32[512]{0:T(512)}, s32[512]{0:T(512)S(1)}, u32[]{:S(2)}) copy-start(s32[512]{0:T(512)S(1)} %iota_add_fusion) | copy-start | bytes 6148
  276.9 7.4 %copy-start.11 = (s32[512]{0:T(512)S(1)}, s32[512]{0:T(512)}, u32[]{:S(2)}) copy-start(s32[512]{0:T(512)} %param.7) | copy-start | bytes 6148
  284.4 1.0 copy-start.19
  285.4 22.0 %copy-start.3 = (bf16[512,1152]{1,0:T(8,128)(2,1)S(1)}, bf16[512,1152]{1,0:T(8,128)(2,1)}, u32[]{:S(2)}) copy-start(bf16[512,1152]{1,0:T(8,128)(2,1)} %copy-done.2) | copy-start | bytes 3538948
  285.4 22.0 %copy-start.18 = (f32[512,512]{1,0:T(8,128)S(1)}, f32[512,512]{1,0:T(8,128)}, u32[]{:S(2)}) copy-start(f32[512,512]{1,0:T(8,128)} %copy-done.17) | copy-start | bytes 3145732
  304.0 30.8 %copy-start.13 = (f32[512,512]{1,0:T(8,128)S(1)}, f32[512,512]{1,0:T(8,128)}, u32[]{:S(2)}) copy-start(f32[512,512]{1,0:T(8,128)} %copy-done.12) | copy-start | bytes 3145732
  304.0 30.8 %collective-permute-start.8 = (f32[512,1152]{1,0:T(8,128)S(1)}, f32[512,1152]{1,0:T(8,128)}, u32[]{:S(2)}, u32[]{:S(2)}) collective-permute-start(f32[512,1152]{1,0:T(8,128)S(1)} %add.254), channel_id=1, source_target_pairs={{0,248},{8,0},{16,8},{24,16},{32,24},{40,32},{48,40},{56,48},{64,5... | collective-permute-start | bytes 7077896 | tf_op jit(solution)/shard_map/ppermute | solution.py:12
  308.4 28.7 %copy-start.5 = (s32[512]{0:T(512)S(1)}, s32[512]{0:T(512)}, u32[]{:S(2)}) copy-start(s32[512]{0:T(512)} %copy-done.4) | copy-start | bytes 6148
  308.4 28.7 %copy-start.15 = (f32[512,512]{1,0:T(8,128)S(1)}, f32[512,512]{1,0:T(8,128)}, u32[]{:S(2)}) copy-start(f32[512,512]{1,0:T(8,128)} %copy-done.14) | copy-start | bytes 3145732
  334.8 127.7 %collective-permute-start.9 = (f32[512,1152]{1,0:T(8,128)}, f32[512,1152]{1,0:T(8,128)S(1)}, u32[]{:S(2)}, u32[]{:S(2)}) collective-permute-start(f32[512,1152]{1,0:T(8,128)} %collective-permute-done.8), channel_id=1, source_target_pairs={{0,5},{1,6},{2,7},{3,0},{4,1},{5,2},{6,3},{7,4},{8,13},{9,14},{10,... | collective-permute-start | bytes 7077896 | tf_op jit(solution)/shard_map/ppermute | solution.py:12
  337.2 7.0 %copy-start.7 = (s32[512]{0:T(512)S(1)}, s32[512]{0:T(512)}, u32[]{:S(2)}) copy-start(s32[512]{0:T(512)} %copy-done.6) | copy-start | bytes 6148
  344.2 113.0 %copy-start.9 = (s32[512]{0:T(512)S(1)}, s32[512]{0:T(512)}, u32[]{:S(2)}) copy-start(s32[512]{0:T(512)} %copy-done.8) | copy-start | bytes 6148
  460.7 1.9 copy-start
where the time goes:
time: 467 us; the launch traced here: 466 us
  waiting for transfers between devices  272 us (58%)
  blocking collectives  108 us (23%)
  matrix products  40.1 us (9%)
  starting transfers between devices  25.6 us (5%)
  other arithmetic  13.6 us (3%)
  between operations  7.46 us (2%)
    ppermute x10, waiting for transfers between devices, from_behind(): return lax.ppermute(value, axis, pairs)  272 us
    psum x1, blocking collectives, body(): total = lax.psum(total, ('outer', 'inner'))  108 us
    ppermute x10, starting transfers between devices, from_behind(): return lax.ppermute(value, axis, pairs)  25.6 us
    dot_general x5, matrix products, body(): d_image = d_image + jnp.dot(coef, held, preferred_element_type=jnp.float32)  15.3 us
    dot_general x5, matrix products, tile_coef(): jnp.einsum('bd,cd->bc', z_img, z_txt, preferred_element_type=jnp.float32)  14.8 us
    dot_general x5, matrix products, text_terms(): jnp.einsum('bc,bd->cd', coef, z_img, preferred_element_type=jnp.float32)  9.99 us
  transfers between devices with their start and end apart: 10, of which 6 were waited for; matrix products, arithmetic and copies ran while one was open for 8% of the time, Pallas kernels for 0%

commit v1 on v0

v1 whole, which is shorter than its diff:
```python
import functools

import jax
import jax.numpy as jnp
from jax import lax
from jax.experimental import pallas as pl
from jax.experimental.pallas import tpu as pltpu
from jax.sharding import PartitionSpec as P

MESH = pl.DeviceIdType.MESH
CHUNK = 64
STEP = 128
TILE = 256


def kernel(
    image, text, positive_hbm, log_temp, bias, loss, g_image, g_text,
    z, raw, d, inv, acc, terms, positive, load_sem, send_sem, recv_sem, loss_send, loss_recv,
):
    rows, width = image.shape
    chunks = rows // CHUNK
    n_outer, n_inner = lax.axis_size("outer"), lax.axis_size("inner")
    o, i = lax.axis_index("outer"), lax.axis_index("inner")
    p, core = lax.rem(i, 2), lax.rem(o, 2)

    def along(steps):
        return (o, lax.rem(i + steps + n_inner, n_inner))

    partner = (o, i + 1 - 2 * p)

    def across(side):
        return (
            lax.rem(o + 1 - 2 * side + n_outer, n_outer),
            lax.rem(i + core - side + n_inner, n_inner),
        )

    barrier = pltpu.get_barrier_semaphore()
    others = (along(2), along(-2), partner, across(0), across(1))

    group = 2 * n_inner
    pairs = n_outer // 2

    def near(k):
        m = lax.rem(2 * i + core + k, group)
        return (o - core + lax.rem(m, 2), m // 2)

    def far(k):
        return (lax.rem(o + 2 * k, n_outer), i)

    def loop(lower, upper, step):
        lax.fori_loop(lower, upper, lambda k, carry: (step(k), carry)[1], 0)

    def greet(device):
        pl.semaphore_signal(barrier, inc=1, device_id=device, device_id_type=MESH)

    for other in others:
        greet(other)
    loop(1, group, lambda k: greet(near(k)))
    loop(1, pairs, lambda k: greet(far(k)))
    n_greet = len(others) + group - 1 + pairs - 1

    def loading(side, c):
        source = image if side else text
        span = pl.ds(c * CHUNK, CHUNK)
        return pltpu.make_async_copy(source.at[span], raw.at[side, span], load_sem.at[side, c])

    for c in range(chunks):
        for side in (0, 1):
            loading(side, c).start()
    load_positive = pltpu.make_async_copy(positive_hbm, positive, load_sem.at[2, 0])
    load_positive.start()

    def copy(side, source, target, c, kind, device):
        span = pl.ds(c * CHUNK, CHUNK)
        return pltpu.make_async_remote_copy(
            src_ref=z.at[side, source, span],
            dst_ref=z.at[side, target, span],
            send_sem=send_sem.at[side, kind],
            recv_sem=recv_sem.at[side, target, c],
            device_id=device,
            device_id_type=MESH,
        )

    def send_ring(side, c):
        copy(side, 0, 2, c, 0, along(2 - 4 * side)).start()

    def send_partner(side, source, c):
        copy(side, source, 1, c, 1, partner).start()

    def send_on(side, c):
        copy(side, 1, 3, c, 2, along(2 - 4 * side)).start()

    def send_cross(side, source, c):
        copy(side, source, 4, c, 3, across(side)).start()

    def arrived(side, slot, c):
        copy(side, slot, slot, c, 0, partner).wait_recv()

    def normalize(side, c):
        span = pl.ds(c * CHUNK, CHUNK)
        x = raw[side, span].astype(jnp.float32)
        scale = lax.rsqrt(jnp.sum(x * x, axis=1, keepdims=True) + 1e-06)
        inv[side, span] = jnp.broadcast_to(scale, (CHUNK, 128))
        z[side, 0, span] = (x * scale).astype(jnp.bfloat16)

    for c in range(chunks):
        for side in (0, 1):
            loading(side, c).wait()
            normalize(side, c)
            if c == 0 and side == 0:
                pl.semaphore_wait(barrier, n_greet)
            send_ring(side, c)

            @pl.when(p == side)
            def _():
                send_partner(side, 0, c)

    temp = jnp.exp(jnp.full((1, 128), log_temp[0], jnp.float32))[:, :1]
    shift = bias[0]

    def sigmoid_parts(logit):
        e = jnp.exp(-jnp.abs(logit))
        r = 1.0 / (1.0 + e)
        return e, jnp.where(logit >= 0.0, r, e * r)

    def fold(term):
        return jnp.sum(term.reshape(-1, 8, term.shape[1]), axis=0)

    def term_copy(stage, k, device):
        return pltpu.make_async_remote_copy(
            src_ref=terms.at[stage, 0], dst_ref=terms.at[stage, k],
            send_sem=loss_send.at[stage], recv_sem=loss_recv.at[stage],
            device_id=device, device_id_type=MESH,
        )

    def spread(stage, value, count, where):
        terms[stage, 0] = value
        loop(1, count, lambda k: term_copy(stage, k, where(k)).start())

    def gathered(stage, count):
        block = terms.at[stage, pl.ds(1, count - 1)]
        both = pltpu.make_async_remote_copy(
            src_ref=block, dst_ref=block, send_sem=loss_send.at[stage], recv_sem=loss_recv.at[stage],
            device_id=partner, device_id_type=MESH,
        )
        both.wait_recv()
        both.wait_send()
        return jnp.sum(terms[stage, :count], axis=0)

    base = (o * n_inner + i) * rows
    acc[...] = jnp.zeros_like(acc)
    load_positive.wait()

    def own_tile(n, carry):
        span = pl.ds(pl.multiple_of(n * STEP, STEP), STEP)
        scores = lax.dot_general(
            z[0, 0, span], z[1, 0], (((1,), (1,)), ((), ())), preferred_element_type=jnp.float32
        )
        logit = temp * scores + shift
        label = positive[...] - (base + n * STEP) == lax.broadcasted_iota(jnp.int32, scores.shape, 0)
        e, sig = sigmoid_parts(logit)
        term = jnp.maximum(logit, 0.0) + jnp.log1p(e) - jnp.where(label, logit, 0.0)
        folded = fold(term)
        acc[...] += sum(folded[:, k * STEP:(k + 1) * STEP] for k in range(rows // STEP))
        coef = (sig - label.astype(jnp.float32)).astype(jnp.bfloat16)
        d[0, span] = jnp.dot(coef, z[1, 0], preferred_element_type=jnp.float32)
        add = lax.dot_general(
            coef, z[0, 0, span], (((0,), (0,)), ((), ())), preferred_element_type=jnp.float32
        )

        @pl.when(n == 0)
        def _():
            d[1] = add

        @pl.when(n > 0)
        def _():
            d[1] += add

        return carry

    lax.fori_loop(0, rows // STEP, own_tile, 0)

    def tile(side, slot, n):
        span = pl.ds(pl.multiple_of(n * STEP, STEP), STEP)
        weight = jnp.where(side == 0, 1.0, 0.0)

        def part(k, carry):
            own = pl.ds(pl.multiple_of(k * TILE, TILE), TILE)
            scores = lax.dot_general(
                z[1 - side, 0, own], z[side, slot, span], (((1,), (1,)), ((), ())),
                preferred_element_type=jnp.float32,
            )
            logit = temp * scores + shift
            e, sig = sigmoid_parts(logit)
            acc[...] += weight * fold(jnp.maximum(logit, 0.0) + jnp.log1p(e))
            d[1 - side, own] += jnp.dot(
                sig.astype(jnp.bfloat16), z[side, slot, span], preferred_element_type=jnp.float32
            )
            return carry

        lax.fori_loop(0, rows // TILE, part, 0)

    per = STEP // CHUNK

    def take_ring(side, c):
        arrived(side, 2, c)

        @pl.when(p != side)
        def _():
            send_partner(side, 2, c)

        @pl.when(core != side)
        def _():
            send_cross(side, 2, c)

    def take_last(side, c):
        arrived(side, 3, c)

        @pl.when(core == side)
        def _():
            send_cross(side, 3, c)

    def take_partner(side, c):
        arrived(side, 1, c)
        send_on(side, c)

    early, late = 1 - p, p

    def first(n, carry):
        for k in range(per):
            c = n * per + k
            take_ring(0, c)
            take_ring(1, c)
            take_partner(early, c)
        tile(0, 2, n)
        tile(1, 2, n)
        tile(early, 1, n)
        return carry

    lax.fori_loop(0, rows // STEP, first, 0)

    def second(n, carry):
        for k in range(per):
            c = n * per + k
            take_partner(late, c)
            take_last(early, c)
        tile(late, 1, n)
        tile(early, 3, n)
        for k in range(per):
            c = n * per + k
            take_last(late, c)
        tile(late, 3, n)
        for side in (0, 1):
            for k in range(per):
                arrived(side, 4, n * per + k)
            tile(side, 4, n)
            if side == 0:

                @pl.when(n == rows // STEP - 1)
                def _():
                    spread(0, acc[...], group, near)

        return carry

    lax.fori_loop(0, rows // STEP, second, 0)

    spread(1, gathered(0, group), pairs, far)

    def finish(c, carry):
        span = pl.ds(pl.multiple_of(c * CHUNK, CHUNK), CHUNK)
        for side, out in ((0, g_text), (1, g_image)):
            scale = inv[side, span][:, :1]
            zn = raw[side, span].astype(jnp.float32) * scale
            grad = temp * d[side, span]
            out[span] = (grad - zn * jnp.sum(zn * grad, axis=1, keepdims=True)) * scale
        return carry

    lax.fori_loop(0, chunks, finish, 0)

    for side in (0, 1):
        for kind in range(4):
            pltpu.make_async_remote_copy(
                src_ref=z.at[side, 0], dst_ref=z.at[side, 0],
                send_sem=send_sem.at[side, kind], recv_sem=recv_sem.at[side, 0, 0],
                device_id=partner, device_id_type=MESH,
            ).wait_send()

    loss[0] = jnp.sum(gathered(1, pairs)) / (rows * n_outer * n_inner)


def body(image_emb, text_emb, positive, log_temp, bias):
    rows, width = image_emb.shape
    chunks = rows // CHUNK
    vmem, smem, anywhere = (pl.BlockSpec(memory_space=m) for m in (pltpu.VMEM, pltpu.SMEM, pl.ANY))
    flops = 2 * 19 * rows * rows * width
    return pl.pallas_call(
        kernel,
        out_shape=(
            jax.ShapeDtypeStruct((1,), jnp.float32),
            jax.ShapeDtypeStruct((rows, width), jnp.float32),
            jax.ShapeDtypeStruct((rows, width), jnp.float32),
        ),
        in_specs=[anywhere, anywhere, anywhere, smem, smem],
        out_specs=(smem, vmem, vmem),
        scratch_shapes=[
            pltpu.VMEM((2, 5, rows, width), jnp.bfloat16),
            pltpu.VMEM((2, rows, width), jnp.bfloat16),
            pltpu.VMEM((2, rows, width), jnp.float32),
            pltpu.VMEM((2, rows, 128), jnp.float32),
            pltpu.VMEM((8, STEP), jnp.float32),
            pltpu.VMEM((2, 16, 8, STEP), jnp.float32),
            pltpu.VMEM((1, rows), jnp.int32),
            pltpu.SemaphoreType.DMA((3, chunks)),
            pltpu.SemaphoreType.DMA((2, 4)),
            pltpu.SemaphoreType.DMA((2, 5, chunks)),
            pltpu.SemaphoreType.DMA((2,)),
            pltpu.SemaphoreType.DMA((2,)),
        ],
        compiler_params=pltpu.CompilerParams(
            collective_id=0, has_side_effects=True, vmem_limit_bytes=60 * 2**20
        ),
        cost_estimate=pl.CostEstimate(
            flops=flops, bytes_accessed=12 * rows * width, transcendentals=27 * rows * rows
        ),
        name="exchange",
    )(image_emb, text_emb, positive.reshape(1, rows), log_temp, bias)


def solution(mesh):
    placed = (
        P(("outer", "inner"), None),
        P(("outer", "inner"), None),
        P(("outer", "inner")),
        P(),
        P(),
    )
    return jax.shard_map(
        body,
        mesh=mesh,
        in_specs=placed,
        out_specs=(P(), P(("outer", "inner"), None), P(("outer", "inner"), None)),
        check_vma=False,
    )
```

time: 467 us -> 124 us (0.27)
  waiting for transfers between devices: 272 us -> 0 us
  Pallas kernels: 0 us -> 115 us
  blocking collectives: 108 us -> 0 us
  matrix products: 40.1 us -> 0 us
  starting transfers between devices: 25.6 us -> 0 us
  other arithmetic: 13.6 us -> 0 us
  local copies, waits for them, and re-layouts: 0.09 us -> 4.78 us
    ppermute x10 -> x0, waiting for transfers between devices: 272 us -> none  [from_behind(): return lax.ppermute(value, axis, pairs)]
    pallas_call x0 -> x1, Pallas kernels: none -> 115 us  [body(): pl.pallas_call(kernel, out_shape=(jax.ShapeDtypeStruct((1,), jnp.float32)...]
    psum x1 -> x0, blocking collectives: 108 us -> none  [body(): total = lax.psum(total, ('outer', 'inner'))]
    dot_general x15 -> x0, matrix products: 40.1 us -> none  [the longest x5 15.3 us: body(): d_image = d_image + jnp.dot(coef, held, preferred_element_type=jnp.float32)]
    ppermute x10 -> x0, starting transfers between devices: 25.6 us -> none  [from_behind(): return lax.ppermute(value, axis, pairs)]
    add x8 -> x0, other arithmetic: 5.7 us -> none  [the longest x3 5.69 us: body(): carried = carried + text_terms(coef, z_img)]
    unnamed x40 -> x4, local copies, waits for them, and re-layouts: 0.09 us -> 4.78 us
  transfers between devices with their start and end apart: 10 -> 0, of which waited for: 6 -> 0; matrix products, arithmetic and copies ran while one was open for 8% -> 0% of each run, Pallas kernels for 0% -> 0%
where the time goes in v1:
time: 124 us
  Pallas kernels  115 us (93%)
  local copies, waits for them, and re-layouts  4.78 us (4%)
  between operations  3.74 us (3%)
    pallas_call x1, Pallas kernels, body(): pl.pallas_call(kernel, out_shape=(jax.ShapeDtypeStruct((1,), jnp.float32)...  115 us
    unnamed x4, local copies, waits for them, and re-layouts  4.78 us

profile of v1, /device:TPU:1, one launch (start us, length us, event | category | flops | bytes accessed | tf_op | source)
XLA Modules:
  0.0 123.5 jit_solution(4210213103709811689)
XLA Ops:
  1.9 115.0 %exchange.1 = (f32[1]{0:T(128)}, f32[512,1152]{1,0:T(8,128)}, f32[512,1152]{1,0:T(8,128)}) custom-call(bf16[512,1152]{1,0:T(8,128)(2,1)} %image.1, bf16[512,1152]{1,0:T(8,128)(2,1)} %text.1, s32[1,512]{1,0:T(1,128)} %bitcast.1, f32[1]{0:T(128)S(6)} %copy.11.log_temp, f32[1]{0:T(128)S(6)} %copy.12.bias), custom_call_target="tpu_custom_call" | custom-call | flops 11475615744 | bytes 7077888 | tf_op jit(solution)/shard_map/exchange/pallas_call | solution.py:296
  117.6 0.0 copy-start
  117.6 3.4 %copy.14 = f32[512,1152]{1,0:T(8,128)} copy(f32[512,1152]{1,0:T(8,128)} %get-tuple-element.7) | data formatting | bytes 4718592
  121.0 0.0 copy-done
  121.0 1.4 %copy.15 = f32[512,1152]{1,0:T(8,128)} copy(f32[512,1152]{1,0:T(8,128)S(1)} %copy-done) | data formatting | bytes 4718592
Async XLA Ops:
  117.6 3.4 %copy-start = (f32[512,1152]{1,0:T(8,128)S(1)}, f32[512,1152]{1,0:T(8,128)}, u32[]{:S(2)}) copy-start(f32[512,1152]{1,0:T(8,128)} %get-tuple-element.8) | copy-start | bytes 7077892

commit v2 on v1

--- a/solution.py
+++ b/solution.py
@@ -9,8 +9,9 @@
 
 MESH = pl.DeviceIdType.MESH
 CHUNK = 64
-STEP = 128
-TILE = 256
+WIDE, NARROW = 256, 128
+HELD = 2
+SPLIT = 4
 
 
 def kernel(
@@ -35,7 +36,9 @@
         )
 
     barrier = pltpu.get_barrier_semaphore()
-    others = (along(2), along(-2), partner, across(0), across(1))
+    sibling = (o + 1 - 2 * core, i)
+    beside = (lax.rem(o + 2 * core - 1 + n_outer, n_outer), i)
+    others = (along(2), along(-2), partner, across(0), across(1), beside, sibling)
 
     group = 2 * n_inner
     pairs = n_outer // 2
@@ -93,6 +96,12 @@
     def send_cross(side, source, c):
         copy(side, source, 4, c, 3, across(side)).start()
 
+    def send_beside(side, c):
+        copy(side, 3, 4, c, 4, beside).start()
+
+    def send_sibling(c):
+        copy(0, 1, 5, c, 5, sibling).start()
+
     def arrived(side, slot, c):
         copy(side, slot, slot, c, 0, partner).wait_recv()
 
@@ -110,11 +119,13 @@
             if c == 0 and side == 0:
                 pl.semaphore_wait(barrier, n_greet)
             send_ring(side, c)
-
-            @pl.when(p == side)
-            def _():
-                send_partner(side, 0, c)
-
+            if side == 0 or c < HELD:
+
+                @pl.when(p == side)
+                def _():
+                    send_partner(side, 0, c)
+
+    load_positive.wait()
     temp = jnp.exp(jnp.full((1, 128), log_temp[0], jnp.float32))[:, :1]
     shift = bias[0]
 
@@ -124,7 +135,8 @@
         return e, jnp.where(logit >= 0.0, r, e * r)
 
     def fold(term):
-        return jnp.sum(term.reshape(-1, 8, term.shape[1]), axis=0)
+        rest = jnp.sum(term.reshape(-1, 8, term.shape[1]), axis=0)
+        return sum(rest[:, k:k + 128] for k in range(0, term.shape[1], 128))
 
     def term_copy(stage, k, device):
         return pltpu.make_async_remote_copy(
@@ -149,19 +161,17 @@
 
     base = (o * n_inner + i) * rows
     acc[...] = jnp.zeros_like(acc)
-    load_positive.wait()
 
     def own_tile(n, carry):
-        span = pl.ds(pl.multiple_of(n * STEP, STEP), STEP)
+        span = pl.ds(pl.multiple_of(n * WIDE, WIDE), WIDE)
         scores = lax.dot_general(
             z[0, 0, span], z[1, 0], (((1,), (1,)), ((), ())), preferred_element_type=jnp.float32
         )
         logit = temp * scores + shift
-        label = positive[...] - (base + n * STEP) == lax.broadcasted_iota(jnp.int32, scores.shape, 0)
+        label = positive[...] - (base + n * WIDE) == lax.broadcasted_iota(jnp.int32, scores.shape, 0)
         e, sig = sigmoid_parts(logit)
         term = jnp.maximum(logit, 0.0) + jnp.log1p(e) - jnp.where(label, logit, 0.0)
-        folded = fold(term)
-        acc[...] += sum(folded[:, k * STEP:(k + 1) * STEP] for k in range(rows // STEP))
+        acc[...] += fold(term)
         coef = (sig - label.astype(jnp.float32)).astype(jnp.bfloat16)
         d[0, span] = jnp.dot(coef, z[1, 0], preferred_element_type=jnp.float32)
         add = lax.dot_general(
@@ -178,29 +188,32 @@
 
         return carry
 
-    lax.fori_loop(0, rows // STEP, own_tile, 0)
-
-    def tile(side, slot, n):
-        span = pl.ds(pl.multiple_of(n * STEP, STEP), STEP)
-        weight = jnp.where(side == 0, 1.0, 0.0)
-
-        def part(k, carry):
-            own = pl.ds(pl.multiple_of(k * TILE, TILE), TILE)
-            scores = lax.dot_general(
-                z[1 - side, 0, own], z[side, slot, span], (((1,), (1,)), ((), ())),
-                preferred_element_type=jnp.float32,
-            )
-            logit = temp * scores + shift
-            e, sig = sigmoid_parts(logit)
-            acc[...] += weight * fold(jnp.maximum(logit, 0.0) + jnp.log1p(e))
-            d[1 - side, own] += jnp.dot(
-                sig.astype(jnp.bfloat16), z[side, slot, span], preferred_element_type=jnp.float32
-            )
-            return carry
-
-        lax.fori_loop(0, rows // TILE, part, 0)
-
-    per = STEP // CHUNK
+    lax.fori_loop(0, rows // WIDE, own_tile, 0)
+
+    def softplus(logit, e):
+        return fold(jnp.maximum(logit, 0.0) + jnp.log1p(e))
+
+    def tile(side, slot, n, size, weight=None):
+        span = pl.ds(pl.multiple_of(n * size, size), size)
+        scores = lax.dot_general(
+            z[1 - side, 0], z[side, slot, span], (((1,), (1,)), ((), ())),
+            preferred_element_type=jnp.float32,
+        )
+        logit = temp * scores + shift
+        e, sig = sigmoid_parts(logit)
+        if weight is not None:
+            acc[...] += weight * softplus(logit, e)
+        d[1 - side] += jnp.dot(
+            sig.astype(jnp.bfloat16), z[side, slot, span], preferred_element_type=jnp.float32
+        )
+
+    def loss_tile(slot, n):
+        span = pl.ds(pl.multiple_of(n * WIDE, WIDE), WIDE)
+        scores = lax.dot_general(
+            z[1, 2], z[0, slot, span], (((1,), (1,)), ((), ())), preferred_element_type=jnp.float32
+        )
+        logit = temp * scores + shift
+        acc[...] += softplus(logit, jnp.exp(-jnp.abs(logit)))
 
     def take_ring(side, c):
         arrived(side, 2, c)
@@ -209,7 +222,7 @@
         def _():
             send_partner(side, 2, c)
 
-        @pl.when(core != side)
+        @pl.when((core != side) & ((p == side) | (c >= SPLIT)))
         def _():
             send_cross(side, 2, c)
 
@@ -219,71 +232,160 @@
         @pl.when(core == side)
         def _():
             send_cross(side, 3, c)
+
+        @pl.when((core != side) & (p == side) & (c < SPLIT))
+        def _():
+            send_beside(side, c)
 
     def take_partner(side, c):
         arrived(side, 1, c)
         send_on(side, c)
 
-    early, late = 1 - p, p
-
-    def first(n, carry):
+    per = NARROW // CHUNK
+    steps = rows // NARROW
+    wide = rows // WIDE
+
+    def take_text(c):
+        take_partner(0, c)
+
+        @pl.when(core == 0)
+        def _():
+            send_sibling(c)
+
+    @functools.partial(loop, 0, steps)
+    def _(n):
         for k in range(per):
             c = n * per + k
             take_ring(0, c)
             take_ring(1, c)
-            take_partner(early, c)
-        tile(0, 2, n)
-        tile(1, 2, n)
-        tile(early, 1, n)
-        return carry
-
-    lax.fori_loop(0, rows // STEP, first, 0)
-
-    def second(n, carry):
+
+            @pl.when(c > 0)
+            def _():
+                take_text(c - 1)
+
+        @pl.when(n == steps - 1)
+        def _():
+            @pl.when(p == 1)
+            def _():
+                loop(HELD, chunks, lambda c: send_partner(1, 0, c))
+
+        @pl.when(lax.rem(n, steps // wide) == steps // wide - 1)
+        def _():
+            tile(0, 2, n // (steps // wide), WIDE, 1.0)
+            tile(1, 2, n // (steps // wide), WIDE)
+
+        @pl.when(n == steps // wide)
+        def _():
+            tile(0, 1, 0, WIDE, 1.0)
+
+    take_text(chunks - 1)
+
+    def plain(n, j):
+        side, slot = jnp.where(j == 1, 0, 1), jnp.where(j == 0, 1, 3)
+
+        @pl.when(((j == 2) & (n > 0)) | ((j < 2) & (n < steps)))
+        def _():
+            tile(side, slot, n - j // 2, NARROW)
+
+    def crossing(side, n, weight=None):
+        n = jnp.where(core == side, lax.rem(n + SPLIT // per, steps), n)
+        for k in range(per):
+            arrived(side, 4, n * per + k)
+        tile(side, 4, n, NARROW, weight)
+
+    @functools.partial(loop, 0, steps + 1)
+    def _(n):
+        @pl.when(n == steps)
+        def _():
+            spread(1, gathered(0, group), pairs, far)
+
         for k in range(per):
             c = n * per + k
-            take_partner(late, c)
-            take_last(early, c)
-        tile(late, 1, n)
-        tile(early, 3, n)
-        for k in range(per):
-            c = n * per + k
-            take_last(late, c)
-        tile(late, 3, n)
-        for side in (0, 1):
-            for k in range(per):
-                arrived(side, 4, n * per + k)
-            tile(side, 4, n)
-            if side == 0:
-
-                @pl.when(n == rows // STEP - 1)
+
+            @pl.when(n < steps)
+            def _():
+                take_partner(1, c)
+                take_last(0, c)
+
+            @pl.when(n > 0)
+            def _():
+                take_last(1, c - per)
+
+            if k == 0:
+
+                @pl.when((n >= core) & (n < steps + core))
+                def _():
+                    crossing(0, n - core, 1.0 - core.astype(jnp.float32))
+
+                @pl.when(n == steps - 1)
                 def _():
                     spread(0, acc[...], group, near)
 
-        return carry
-
-    lax.fori_loop(0, rows // STEP, second, 0)
-
-    spread(1, gathered(0, group), pairs, far)
-
-    def finish(c, carry):
-        span = pl.ds(pl.multiple_of(c * CHUNK, CHUNK), CHUNK)
-        for side, out in ((0, g_text), (1, g_image)):
+                lag = 2 * (1 - core)
+
+                @pl.when((n >= lag) & (n < steps + lag))
+                def _():
+                    crossing(1, n - lag)
+
+        @pl.when(n == 0)
+        def _():
+            tile(0, 1, wide - 1, WIDE, 1.0)
+
+        loop(0, 3, lambda j: plain(n, j))
+
+        @pl.when(n == 0)
+        def _():
+            loop(0, wide, lambda m: loss_tile(1, m))
+
+        @pl.when((n == 1) & (core == 1))
+        def _():
+            loop(0, chunks, lambda c: arrived(0, 5, c))
+            loop(0, wide, lambda m: loss_tile(5, m))
+
+    def finish(side, out):
+        def part(c):
+            span = pl.ds(pl.multiple_of(c * CHUNK, CHUNK), CHUNK)
             scale = inv[side, span][:, :1]
             zn = raw[side, span].astype(jnp.float32) * scale
             grad = temp * d[side, span]
             out[span] = (grad - zn * jnp.sum(zn * grad, axis=1, keepdims=True)) * scale
-        return carry
-
-    lax.fori_loop(0, chunks, finish, 0)
+
+        loop(0, chunks, part)
+
+    finish(1, g_image)
+
+    @pl.when(core == 0)
+    def _():
+        crossing(1, steps - 1)
+
+    finish(0, g_text)
+
+    def sent(side, kind, count):
+        span = z.at[side, 0, pl.ds(0, count * CHUNK)]
+        pltpu.make_async_remote_copy(
+            src_ref=span, dst_ref=span, send_sem=send_sem.at[side, kind], recv_sem=recv_sem.at[side, 0, 0],
+            device_id=partner, device_id_type=MESH,
+        ).wait_send()
 
     for side in (0, 1):
-        for kind in range(4):
-            pltpu.make_async_remote_copy(
-                src_ref=z.at[side, 0], dst_ref=z.at[side, 0],
-                send_sem=send_sem.at[side, kind], recv_sem=recv_sem.at[side, 0, 0],
-                device_id=partner, device_id_type=MESH,
-            ).wait_send()
+        for kind in range(3):
+            sent(side, kind, chunks)
+
+        @pl.when((core == side) | (p == side))
+        def _():
+            sent(side, 3, chunks)
+
+        @pl.when((core != side) & (p != side))
+        def _():
+            sent(side, 3, chunks - SPLIT)
+
+        @pl.when((core != side) & (p == side))
+        def _():
+            sent(side, 4, SPLIT)
+
+    @pl.when(core == 0)
+    def _():
+        sent(0, 5, chunks)
 
     loss[0] = jnp.sum(gathered(1, pairs)) / (rows * n_outer * n_inner)
 
@@ -291,39 +393,40 @@
 def body(image_emb, text_emb, positive, log_temp, bias):
     rows, width = image_emb.shape
     chunks = rows // CHUNK
-    vmem, smem, anywhere = (pl.BlockSpec(memory_space=m) for m in (pltpu.VMEM, pltpu.SMEM, pl.ANY))
-    flops = 2 * 19 * rows * rows * width
+    vmem, smem, hbm = (pl.BlockSpec(memory_space=m) for m in (pltpu.VMEM, pltpu.SMEM, pltpu.HBM))
+    large = (image_emb, text_emb, positive.reshape(1, rows))
+    flops = 2 * 21 * rows * rows * width
     return pl.pallas_call(
         kernel,
         out_shape=(
             jax.ShapeDtypeStruct((1,), jnp.float32),
-            jax.ShapeDtypeStruct((rows, width), jnp.float32),
-            jax.ShapeDtypeStruct((rows, width), jnp.float32),
+            pltpu.VMEM((rows, width), jnp.float32),
+            pltpu.VMEM((rows, width), jnp.float32),
         ),
-        in_specs=[anywhere, anywhere, anywhere, smem, smem],
+        in_specs=[hbm, hbm, hbm, smem, smem],
         out_specs=(smem, vmem, vmem),
         scratch_shapes=[
-            pltpu.VMEM((2, 5, rows, width), jnp.bfloat16),
+            pltpu.VMEM((2, 6, rows, width), jnp.bfloat16),
             pltpu.VMEM((2, rows, width), jnp.bfloat16),
             pltpu.VMEM((2, rows, width), jnp.float32),
             pltpu.VMEM((2, rows, 128), jnp.float32),
-            pltpu.VMEM((8, STEP), jnp.float32),
-            pltpu.VMEM((2, 16, 8, STEP), jnp.float32),
+            pltpu.VMEM((8, 128), jnp.float32),
+            pltpu.VMEM((2, 16, 8, 128), jnp.float32),
             pltpu.VMEM((1, rows), jnp.int32),
             pltpu.SemaphoreType.DMA((3, chunks)),
-            pltpu.SemaphoreType.DMA((2, 4)),
-            pltpu.SemaphoreType.DMA((2, 5, chunks)),
+            pltpu.SemaphoreType.DMA((2, 6)),
+            pltpu.SemaphoreType.DMA((2, 6, chunks)),
             pltpu.SemaphoreType.DMA((2,)),
             pltpu.SemaphoreType.DMA((2,)),
         ],
         compiler_params=pltpu.CompilerParams(
-            collective_id=0, has_side_effects=True, vmem_limit_bytes=60 * 2**20
+            collective_id=0, has_side_effects=True, vmem_limit_bytes=40 * 2**20
         ),
         cost_estimate=pl.CostEstimate(
             flops=flops, bytes_accessed=12 * rows * width, transcendentals=27 * rows * rows
         ),
         name="exchange",
-    )(image_emb, text_emb, positive.reshape(1, rows), log_temp, bias)
+    )(*(pltpu.with_memory_space_constraint(x, pltpu.HBM) for x in large), log_temp, bias)
 
 
 def solution(mesh):

time: 124 us -> 102 us (0.82)
  the two profiles are of different devices: /device:TPU:1 before, /device:TPU:16 now
where the time goes in v2:
time: 102 us
  Pallas kernels  95.1 us (93%)
  between operations  3.62 us (4%)
  local copies, waits for them, and re-layouts  2.81 us (3%)
    pallas_call x1, Pallas kernels, body(): pl.pallas_call(kernel, out_shape=(jax.ShapeDtypeStruct((1,), jnp.float32)...  95.1 us
    unnamed x2, local copies, waits for them, and re-layouts  2.81 us

profile of v2, /device:TPU:16, one launch (start us, length us, event | category | flops | bytes accessed | tf_op | source)
XLA Modules:
  0.0 101.5 jit_solution(8394679861403553946)
XLA Ops:
  1.9 95.1 %exchange.1 = (f32[1]{0:T(128)}, f32[512,1152]{1,0:T(8,128)S(1)}, f32[512,1152]{1,0:T(8,128)S(1)}) custom-call(bf16[512,1152]{1,0:T(8,128)(2,1)} %image.1, bf16[512,1152]{1,0:T(8,128)(2,1)} %text.1, s32[1,512]{1,0:T(1,128)} %bitcast.1, f32[1]{0:T(128)S(6)} %copy.13.log_temp, f32[1]{0:T(128)S(6)} %copy.14.bias), custom_call_target="tpu_custom_call" | custom-call | flops 12683575296 | bytes 7077888 | tf_op jit(solution)/shard_map/exchange/pallas_call | solution.py:399
  97.0 1.4 %copy.11 = f32[512,1152]{1,0:T(8,128)} copy(f32[512,1152]{1,0:T(8,128)S(1)} %get-tuple-element.4) | data formatting | bytes 4718592
  98.4 1.4 %copy.12 = f32[512,1152]{1,0:T(8,128)} copy(f32[512,1152]{1,0:T(8,128)S(1)} %get-tuple-element.5) | data formatting | bytes 4718592

commit v3 on v2

--- a/solution.py
+++ b/solution.py
@@ -37,8 +37,8 @@
 
     barrier = pltpu.get_barrier_semaphore()
     sibling = (o + 1 - 2 * core, i)
-    beside = (lax.rem(o + 2 * core - 1 + n_outer, n_outer), i)
-    others = (along(2), along(-2), partner, across(0), across(1), beside, sibling)
+    between = (lax.rem(o + 2 * core - 1 + n_outer, n_outer), lax.rem(i + 1 - 2 * core + n_inner, n_inner))
+    others = (along(2), along(-2), partner, across(0), across(1), between, sibling)
 
     group = 2 * n_inner
     pairs = n_outer // 2
@@ -96,8 +96,12 @@
     def send_cross(side, source, c):
         copy(side, source, 4, c, 3, across(side)).start()
 
-    def send_beside(side, c):
-        copy(side, 3, 4, c, 4, beside).start()
+    def send_between(side, c):
+        copy(side, 2, 6, c, 4, between).start()
+
+    def pass_on(side, c):
+        arrived(side, 6, c)
+        copy(side, 6, 4, c, 6, along(2 - 4 * side)).start()
 
     def send_sibling(c):
         copy(0, 1, 5, c, 5, sibling).start()
@@ -226,6 +230,10 @@
         def _():
             send_cross(side, 2, c)
 
+        @pl.when((core != side) & (p != side) & (c < SPLIT))
+        def _():
+            send_between(side, c)
+
     def take_last(side, c):
         arrived(side, 3, c)
 
@@ -233,20 +241,16 @@
         def _():
             send_cross(side, 3, c)
 
-        @pl.when((core != side) & (p == side) & (c < SPLIT))
-        def _():
-            send_beside(side, c)
-
-    def take_partner(side, c):
-        arrived(side, 1, c)
-        send_on(side, c)
+    def take_image(c):
+        arrived(1, 1, c)
+        send_on(1, c)
 
     per = NARROW // CHUNK
     steps = rows // NARROW
     wide = rows // WIDE
 
     def take_text(c):
-        take_partner(0, c)
+        arrived(0, 1, c)
 
         @pl.when(core == 0)
         def _():
@@ -263,6 +267,13 @@
             def _():
                 take_text(c - 1)
 
+        for side in (0, 1):
+
+            @pl.when((core == side) & (p == side) & (n > 0) & (n <= SPLIT // per))
+            def _():
+                for k in range(per):
+                    pass_on(side, (n - 1) * per + k)
+
         @pl.when(n == steps - 1)
         def _():
             @pl.when(p == 1)
@@ -278,17 +289,18 @@
         def _():
             tile(0, 1, 0, WIDE, 1.0)
 
+    loop(0, chunks - 1, lambda c: send_on(0, c))
     take_text(chunks - 1)
+    send_on(0, chunks - 1)
 
     def plain(n, j):
         side, slot = jnp.where(j == 1, 0, 1), jnp.where(j == 0, 1, 3)
 
-        @pl.when(((j == 2) & (n > 0)) | ((j < 2) & (n < steps)))
-        def _():
-            tile(side, slot, n - j // 2, NARROW)
+        @pl.when(((j > 0) & (n > 0)) | ((j == 0) & (n < steps)))
+        def _():
+            tile(side, slot, n - jnp.minimum(j, 1), NARROW)
 
     def crossing(side, n, weight=None):
-        n = jnp.where(core == side, lax.rem(n + SPLIT // per, steps), n)
         for k in range(per):
             arrived(side, 4, n * per + k)
         tile(side, 4, n, NARROW, weight)
@@ -304,18 +316,18 @@
 
             @pl.when(n < steps)
             def _():
-                take_partner(1, c)
-                take_last(0, c)
+                take_image(c)
 
             @pl.when(n > 0)
             def _():
+                take_last(0, c - per)
                 take_last(1, c - per)
 
             if k == 0:
 
-                @pl.when((n >= core) & (n < steps + core))
+                @pl.when((n >= 2 * core) & (n < steps + 2 * core))
                 def _():
-                    crossing(0, n - core, 1.0 - core.astype(jnp.float32))
+                    crossing(0, n - 2 * core, 1.0 - core.astype(jnp.float32))
 
                 @pl.when(n == steps - 1)
                 def _():
@@ -352,13 +364,17 @@
 
         loop(0, chunks, part)
 
-    finish(1, g_image)
-
     @pl.when(core == 0)
     def _():
+        finish(1, g_image)
         crossing(1, steps - 1)
-
-    finish(0, g_text)
+        finish(0, g_text)
+
+    @pl.when(core == 1)
+    def _():
+        finish(0, g_text)
+        crossing(0, steps - 1)
+        finish(1, g_image)
 
     def sent(side, kind, count):
         span = z.at[side, 0, pl.ds(0, count * CHUNK)]
@@ -378,10 +394,11 @@
         @pl.when((core != side) & (p != side))
         def _():
             sent(side, 3, chunks - SPLIT)
-
-        @pl.when((core != side) & (p == side))
-        def _():
             sent(side, 4, SPLIT)
+
+        @pl.when((core == side) & (p == side))
+        def _():
+            sent(side, 6, SPLIT)
 
     @pl.when(core == 0)
     def _():
@@ -406,7 +423,7 @@
         in_specs=[hbm, hbm, hbm, smem, smem],
         out_specs=(smem, vmem, vmem),
         scratch_shapes=[
-            pltpu.VMEM((2, 6, rows, width), jnp.bfloat16),
+            pltpu.VMEM((2, 7, rows, width), jnp.bfloat16),
             pltpu.VMEM((2, rows, width), jnp.bfloat16),
             pltpu.VMEM((2, rows, width), jnp.float32),
             pltpu.VMEM((2, rows, 128), jnp.float32),
@@ -414,8 +431,8 @@
             pltpu.VMEM((2, 16, 8, 128), jnp.float32),
             pltpu.VMEM((1, rows), jnp.int32),
             pltpu.SemaphoreType.DMA((3, chunks)),
-            pltpu.SemaphoreType.DMA((2, 6)),
-            pltpu.SemaphoreType.DMA((2, 6, chunks)),
+            pltpu.SemaphoreType.DMA((2, 7)),
+            pltpu.SemaphoreType.DMA((2, 7, chunks)),
             pltpu.SemaphoreType.DMA((2,)),
             pltpu.SemaphoreType.DMA((2,)),
         ],

time: 102 us -> 92.5 us (0.907)
  the two profiles are of different devices: /device:TPU:16 before, /device:TPU:1 now
where the time goes in v3:
time: 92.5 us; the launch traced here: 92.4 us
  Pallas kernels  85.9 us (93%)
  between operations  3.62 us (4%)
  local copies, waits for them, and re-layouts  2.81 us (3%)
    pallas_call x1, Pallas kernels, body(): pl.pallas_call(kernel, out_shape=(jax.ShapeDtypeStruct((1,), jnp.float32)...  85.9 us
    unnamed x2, local copies, waits for them, and re-layouts  2.81 us

profile of v3, /device:TPU:1, one launch (start us, length us, event | category | flops | bytes accessed | tf_op | source)
XLA Modules:
  0.0 92.4 jit_solution(17190871436199552171)
XLA Ops:
  1.9 85.9 %exchange.1 = (f32[1]{0:T(128)}, f32[512,1152]{1,0:T(8,128)S(1)}, f32[512,1152]{1,0:T(8,128)S(1)}) custom-call(bf16[512,1152]{1,0:T(8,128)(2,1)} %image.1, bf16[512,1152]{1,0:T(8,128)(2,1)} %text.1, s32[1,512]{1,0:T(1,128)} %bitcast.1, f32[1]{0:T(128)S(6)} %copy.13.log_temp, f32[1]{0:T(128)S(6)} %copy.14.bias), custom_call_target="tpu_custom_call" | custom-call | flops 12683575296 | bytes 7077888 | tf_op jit(solution)/shard_map/exchange/pallas_call | solution.py:416
  87.9 1.4 %copy.11 = f32[512,1152]{1,0:T(8,128)} copy(f32[512,1152]{1,0:T(8,128)S(1)} %get-tuple-element.4) | data formatting | bytes 4718592
  89.3 1.4 %copy.12 = f32[512,1152]{1,0:T(8,128)} copy(f32[512,1152]{1,0:T(8,128)S(1)} %get-tuple-element.5) | data formatting | bytes 4718592

commit v4 on v3

--- a/solution.py
+++ b/solution.py
@@ -15,8 +15,8 @@
 
 
 def kernel(
-    image, text, positive_hbm, log_temp, bias, loss, g_image, g_text,
-    z, raw, d, inv, acc, terms, positive, load_sem, send_sem, recv_sem, loss_send, loss_recv,
+    image, text, positive_hbm, scalars, total, d, raw, inv,
+    z, acc, terms, positive, load_sem, send_sem, recv_sem, loss_send, loss_recv,
 ):
     rows, width = image.shape
     chunks = rows // CHUNK
@@ -130,8 +130,7 @@
                     send_partner(side, 0, c)
 
     load_positive.wait()
-    temp = jnp.exp(jnp.full((1, 128), log_temp[0], jnp.float32))[:, :1]
-    shift = bias[0]
+    temp, shift = jnp.exp(scalars[0:1, 0:1]), scalars[1:2, 0:1]
 
     def sigmoid_parts(logit):
         e = jnp.exp(-jnp.abs(logit))
@@ -307,10 +306,6 @@
 
     @functools.partial(loop, 0, steps + 1)
     def _(n):
-        @pl.when(n == steps)
-        def _():
-            spread(1, gathered(0, group), pairs, far)
-
         for k in range(per):
             c = n * per + k
 
@@ -324,20 +319,17 @@
                 take_last(1, c - per)
 
             if k == 0:
-
-                @pl.when((n >= 2 * core) & (n < steps + 2 * core))
+                @pl.when((n > 0) & (n <= steps // 2))
                 def _():
-                    crossing(0, n - 2 * core, 1.0 - core.astype(jnp.float32))
-
-                @pl.when(n == steps - 1)
+                    loop(2 * n - 2, 2 * n, lambda m: crossing(core, m, 1.0 - core.astype(jnp.float32)))
+
+                @pl.when(n == steps // 2)
                 def _():
                     spread(0, acc[...], group, near)
 
-                lag = 2 * (1 - core)
-
-                @pl.when((n >= lag) & (n < steps + lag))
+                @pl.when(n >= 2)
                 def _():
-                    crossing(1, n - lag)
+                    crossing(1 - core, n - 2)
 
         @pl.when(n == 0)
         def _():
@@ -345,36 +337,20 @@
 
         loop(0, 3, lambda j: plain(n, j))
 
+        @pl.when(n == steps - 1)
+        def _():
+            spread(1, gathered(0, group), pairs, far)
+
         @pl.when(n == 0)
         def _():
             loop(0, wide, lambda m: loss_tile(1, m))
 
-        @pl.when((n == 1) & (core == 1))
+        @pl.when((n == 0) & (core == 1))
         def _():
             loop(0, chunks, lambda c: arrived(0, 5, c))
             loop(0, wide, lambda m: loss_tile(5, m))
 
-    def finish(side, out):
-        def part(c):
-            span = pl.ds(pl.multiple_of(c * CHUNK, CHUNK), CHUNK)
-            scale = inv[side, span][:, :1]
-            zn = raw[side, span].astype(jnp.float32) * scale
-            grad = temp * d[side, span]
-            out[span] = (grad - zn * jnp.sum(zn * grad, axis=1, keepdims=True)) * scale
-
-        loop(0, chunks, part)
-
-    @pl.when(core == 0)
-    def _():
-        finish(1, g_image)
-        crossing(1, steps - 1)
-        finish(0, g_text)
-
-    @pl.when(core == 1)
-    def _():
-        finish(0, g_text)
-        crossing(0, steps - 1)
-        finish(1, g_image)
+    crossing(1 - core, steps - 1)
 
     def sent(side, kind, count):
         span = z.at[side, 0, pl.ds(0, count * CHUNK)]
@@ -404,7 +380,25 @@
     def _():
         sent(0, 5, chunks)
 
-    loss[0] = jnp.sum(gathered(1, pairs)) / (rows * n_outer * n_inner)
+    total[...] = gathered(1, pairs)
+
+
+def finish(images, scalars, total, d, raw, inv, loss, g_image, g_text, grads, sems):
+    rows = d.shape[1]
+    temp = jnp.exp(scalars[0:1, 0:1])
+    copies = []
+    for c in range(rows // NARROW):
+        span = pl.ds(c * NARROW, NARROW)
+        for side, out in ((0, g_text), (1, g_image)):
+            scale = inv[side, span][:, :1]
+            zn = raw[side, span].astype(jnp.float32) * scale
+            grad = temp * d[side, span]
+            grads[side, span] = (grad - zn * jnp.sum(zn * grad, axis=1, keepdims=True)) * scale
+            copies.append(pltpu.make_async_copy(grads.at[side, span], out.at[span], sems.at[side, c]))
+            copies[-1].start()
+    loss[0] = jnp.sum(total[...]) / images
+    for copy in copies:
+        copy.wait()
 
 
 def body(image_emb, text_emb, positive, log_temp, bias):
@@ -412,21 +406,20 @@
     chunks = rows // CHUNK
     vmem, smem, hbm = (pl.BlockSpec(memory_space=m) for m in (pltpu.VMEM, pltpu.SMEM, pltpu.HBM))
     large = (image_emb, text_emb, positive.reshape(1, rows))
-    flops = 2 * 21 * rows * rows * width
-    return pl.pallas_call(
+    row = lax.broadcasted_iota(jnp.int32, (8, 128), 0)
+    scalars = jnp.where(row == 0, log_temp[0], bias[0])
+    sums = pl.pallas_call(
         kernel,
         out_shape=(
-            jax.ShapeDtypeStruct((1,), jnp.float32),
-            pltpu.VMEM((rows, width), jnp.float32),
-            pltpu.VMEM((rows, width), jnp.float32),
+            pltpu.VMEM((8, 128), jnp.float32),
+            pltpu.VMEM((2, rows, width), jnp.float32),
+            pltpu.VMEM((2, rows, width), jnp.bfloat16),
+            pltpu.VMEM((2, rows, 128), jnp.float32),
         ),
-        in_specs=[hbm, hbm, hbm, smem, smem],
-        out_specs=(smem, vmem, vmem),
+        in_specs=[hbm, hbm, hbm, vmem],
+        out_specs=(vmem,) * 4,
         scratch_shapes=[
             pltpu.VMEM((2, 7, rows, width), jnp.bfloat16),
-            pltpu.VMEM((2, rows, width), jnp.bfloat16),
-            pltpu.VMEM((2, rows, width), jnp.float32),
-            pltpu.VMEM((2, rows, 128), jnp.float32),
             pltpu.VMEM((8, 128), jnp.float32),
             pltpu.VMEM((2, 16, 8, 128), jnp.float32),
             pltpu.VMEM((1, rows), jnp.int32),
@@ -440,10 +433,27 @@
             collective_id=0, has_side_effects=True, vmem_limit_bytes=40 * 2**20
         ),
         cost_estimate=pl.CostEstimate(
-            flops=flops, bytes_accessed=12 * rows * width, transcendentals=27 * rows * rows
+            flops=2 * 21 * rows * rows * width, bytes_accessed=4 * rows * width, transcendentals=27 * rows * rows
         ),
         name="exchange",
-    )(*(pltpu.with_memory_space_constraint(x, pltpu.HBM) for x in large), log_temp, bias)
+    )(*(pltpu.with_memory_space_constraint(x, pltpu.HBM) for x in large), scalars)
+    images = rows * lax.axis_size("outer") * lax.axis_size("inner")
+    grad = jax.ShapeDtypeStruct((rows, width), jnp.float32)
+    return pl.pallas_call(
+        functools.partial(finish, images),
+        out_shape=(jax.ShapeDtypeStruct((1,), jnp.float32), grad, grad),
+        in_specs=[vmem] * 5,
+        out_specs=(smem, hbm, hbm),
+        scratch_shapes=[
+            pltpu.VMEM((2, rows, width), jnp.float32),
+            pltpu.SemaphoreType.DMA((2, chunks)),
+        ],
+        compiler_params=pltpu.CompilerParams(vmem_limit_bytes=16 * 2**20),
+        cost_estimate=pl.CostEstimate(
+            flops=14 * rows * width, bytes_accessed=8 * rows * width, transcendentals=0
+        ),
+        name="finish",
+    )(scalars, *sums)
 
 
 def solution(mesh):

time: 92.5 us -> 87.7 us (0.948)
  local copies, waits for them, and re-layouts: 2.81 us -> 0.07 us
  between operations: 3.62 us -> 2.1 us
    unnamed x2 -> x0, local copies, waits for them, and re-layouts: 2.81 us -> none
    pallas_call x1 -> x2, Pallas kernels: 85.9 us -> 85.4 us  [the longest x1 82.2 us: body(): pl.pallas_call(kernel, out_shape=(pltpu.VMEM((8, 128), jnp.float32), pltp...]
where the time goes in v4:
time: 87.7 us; the launch traced here: 87.6 us
  Pallas kernels  85.4 us (97%)
  between operations  2.1 us (2%)
    pallas_call x1, Pallas kernels, body(): pl.pallas_call(kernel, out_shape=(pltpu.VMEM((8, 128), jnp.float32), pltp...  82.2 us
    pallas_call x1, Pallas kernels, body(): pl.pallas_call(functools.partial(finish, images), out_shape=(jax.ShapeDty...  3.23 us

profile of v4, /device:TPU:1, one launch (start us, length us, event | category | flops | bytes accessed | tf_op | source)
XLA Modules:
  0.0 87.6 jit_solution(8530399386910586057)
XLA Ops:
  1.9 0.1 iota.7.scalars
  2.0 82.2 %exchange.1 = (f32[8,128]{1,0:T(8,128)S(1)}, f32[2,512,1152]{2,1,0:T(8,128)S(1)}, bf16[2,512,1152]{2,1,0:T(8,128)(2,1)S(1)}, f32[2,512,128]{2,1,0:T(8,128)S(1)}) custom-call(bf16[512,1152]{1,0:T(8,128)(2,1)} %image.1, bf16[512,1152]{1,0:T(8,128)(2,1)} %text.1, s32[1,512]{1,0:T(1,128)} %bitcast.5, f32[8,128]{1,0:T(8,128)S(1)} %iota.7.scalars), custom_call_target="tpu_custom_call" | custom-call | flops 12683575296 | bytes 2359296 | tf_op jit(solution)/shard_map/exchange/pallas_call | solution.py:411
  84.2 3.2 %finish.1 = (f32[1]{0:T(128)}, f32[512,1152]{1,0:T(8,128)}, f32[512,1152]{1,0:T(8,128)}) custom-call(f32[8,128]{1,0:T(8,128)S(1)} %iota.7.scalars, f32[8,128]{1,0:T(8,128)S(1)} %get-tuple-element.7.total, f32[2,512,1152]{2,1,0:T(8,128)S(1)} %get-tuple-element.8.d, bf16[2,512,1152]{2,1,0:T(8,128)(2,1)S(1)} %get-tuple-element.9.raw, ...), custom_call_target="tpu_custom_call" | custom-call | flops 8257536 | bytes 4718592 | tf_op jit(solution)/shard_map/finish/pallas_call | solution.py:442
  (1 shorter events, 0.0 us)

commit v5 on v4

--- a/solution.py
+++ b/solution.py
@@ -35,6 +35,17 @@
             lax.rem(i + core - side + n_inner, n_inner),
         )
 
+    def loading(side, c):
+        source = image if side else text
+        span = pl.ds(c * CHUNK, CHUNK)
+        return pltpu.make_async_copy(source.at[span], raw.at[side, span], load_sem.at[side, c])
+
+    for c in range(chunks):
+        for side in (0, 1):
+            loading(side, c).start()
+    load_positive = pltpu.make_async_copy(positive_hbm, positive, load_sem.at[2, 0])
+    load_positive.start()
+
     barrier = pltpu.get_barrier_semaphore()
     sibling = (o + 1 - 2 * core, i)
     between = (lax.rem(o + 2 * core - 1 + n_outer, n_outer), lax.rem(i + 1 - 2 * core + n_inner, n_inner))
@@ -61,17 +72,6 @@
     loop(1, group, lambda k: greet(near(k)))
     loop(1, pairs, lambda k: greet(far(k)))
     n_greet = len(others) + group - 1 + pairs - 1
-
-    def loading(side, c):
-        source = image if side else text
-        span = pl.ds(c * CHUNK, CHUNK)
-        return pltpu.make_async_copy(source.at[span], raw.at[side, span], load_sem.at[side, c])
-
-    for c in range(chunks):
-        for side in (0, 1):
-            loading(side, c).start()
-    load_positive = pltpu.make_async_copy(positive_hbm, positive, load_sem.at[2, 0])
-    load_positive.start()
 
     def copy(side, source, target, c, kind, device):
         span = pl.ds(c * CHUNK, CHUNK)
@@ -198,17 +198,17 @@
 
     def tile(side, slot, n, size, weight=None):
         span = pl.ds(pl.multiple_of(n * size, size), size)
+        meet(side, z[side, slot, span], weight)
+
+    def meet(side, block, weight=None):
         scores = lax.dot_general(
-            z[1 - side, 0], z[side, slot, span], (((1,), (1,)), ((), ())),
-            preferred_element_type=jnp.float32,
+            z[1 - side, 0], block, (((1,), (1,)), ((), ())), preferred_element_type=jnp.float32
         )
         logit = temp * scores + shift
         e, sig = sigmoid_parts(logit)
         if weight is not None:
             acc[...] += weight * softplus(logit, e)
-        d[1 - side] += jnp.dot(
-            sig.astype(jnp.bfloat16), z[side, slot, span], preferred_element_type=jnp.float32
-        )
+        d[1 - side] += jnp.dot(sig.astype(jnp.bfloat16), block, preferred_element_type=jnp.float32)
 
     def loss_tile(slot, n):
         span = pl.ds(pl.multiple_of(n * WIDE, WIDE), WIDE)
@@ -295,7 +295,7 @@
     def plain(n, j):
         side, slot = jnp.where(j == 1, 0, 1), jnp.where(j == 0, 1, 3)
 
-        @pl.when(((j > 0) & (n > 0)) | ((j == 0) & (n < steps)))
+        @pl.when(jnp.where(j == 0, n < steps, (n > 0) & ((n < steps) | (side == core))))
         def _():
             tile(side, slot, n - jnp.minimum(j, 1), NARROW)
 
@@ -350,7 +350,10 @@
             loop(0, chunks, lambda c: arrived(0, 5, c))
             loop(0, wide, lambda m: loss_tile(5, m))
 
-    crossing(1 - core, steps - 1)
+    for k in range(per):
+        arrived(1 - core, 4, chunks - per + k)
+    span = pl.ds(rows - NARROW, NARROW)
+    meet(1 - core, jnp.concatenate([z[1 - core, 3, span], z[1 - core, 4, span]], axis=0))
 
     def sent(side, kind, count):
         span = z.at[side, 0, pl.ds(0, count * CHUNK)]

time: 87.7 us -> 87.1 us (level)
  no operation moved by 1% of the time
where the time goes in v5:
time: 87.1 us; the launch traced here: 86.8 us
  Pallas kernels  84.6 us (97%)
  between operations  2.1 us (2%)
    pallas_call x1, Pallas kernels, body(): pl.pallas_call(kernel, out_shape=(pltpu.VMEM((8, 128), jnp.float32), pltp...  81.4 us
    pallas_call x1, Pallas kernels, body(): pl.pallas_call(functools.partial(finish, images), out_shape=(jax.ShapeDty...  3.23 us

profile of v5, /device:TPU:1, one launch (start us, length us, event | category | flops | bytes accessed | tf_op | source)
XLA Modules:
  0.0 86.8 jit_solution(669831983135277269)
XLA Ops:
  1.9 0.1 iota.7.scalars
  2.0 81.4 %exchange.1 = (f32[8,128]{1,0:T(8,128)S(1)}, f32[2,512,1152]{2,1,0:T(8,128)S(1)}, bf16[2,512,1152]{2,1,0:T(8,128)(2,1)S(1)}, f32[2,512,128]{2,1,0:T(8,128)S(1)}) custom-call(bf16[512,1152]{1,0:T(8,128)(2,1)} %image.1, bf16[512,1152]{1,0:T(8,128)(2,1)} %text.1, s32[1,512]{1,0:T(1,128)} %bitcast.5, f32[8,128]{1,0:T(8,128)S(1)} %iota.7.scalars), custom_call_target="tpu_custom_call" | custom-call | flops 12683575296 | bytes 2359296 | tf_op jit(solution)/shard_map/exchange/pallas_call | solution.py:414
  83.4 3.2 %finish.1 = (f32[1]{0:T(128)}, f32[512,1152]{1,0:T(8,128)}, f32[512,1152]{1,0:T(8,128)}) custom-call(f32[8,128]{1,0:T(8,128)S(1)} %iota.7.scalars, f32[8,128]{1,0:T(8,128)S(1)} %get-tuple-element.7.total, f32[2,512,1152]{2,1,0:T(8,128)S(1)} %get-tuple-element.8.d, bf16[2,512,1152]{2,1,0:T(8,128)(2,1)S(1)} %get-tuple-element.9.raw, ...), custom_call_target="tpu_custom_call" | custom-call | flops 8257536 | bytes 4718592 | tf_op jit(solution)/shard_map/finish/pallas_call | solution.py:445
  (1 shorter events, 0.0 us)

commit v6 on v5

--- a/solution.py
+++ b/solution.py
@@ -295,7 +295,9 @@
     def plain(n, j):
         side, slot = jnp.where(j == 1, 0, 1), jnp.where(j == 0, 1, 3)
 
-        @pl.when(jnp.where(j == 0, n < steps, (n > 0) & ((n < steps) | (side == core))))
+        last = (n == steps) & (side == core)
+
+        @pl.when(jnp.where(j == 0, n == 0, last | ((j == 1) & (n > 0) & (n < steps))))
         def _():
             tile(side, slot, n - jnp.minimum(j, 1), NARROW)
 
@@ -336,6 +338,11 @@
             tile(0, 1, wide - 1, WIDE, 1.0)
 
         loop(0, 3, lambda j: plain(n, j))
+
+        @pl.when((n > 0) & (n < steps))
+        def _():
+            one, three = (pl.ds(pl.multiple_of((n - k) * NARROW, NARROW), NARROW) for k in (0, 1))
+            meet(1, jnp.concatenate([z[1, 1, one], z[1, 3, three]], axis=0))
 
         @pl.when(n == steps - 1)
         def _():

time: 87.1 us -> 86.7 us (level)
  no operation moved by 1% of the time
where the time goes in v6:
time: 86.7 us; the launch traced here: 86.6 us
  Pallas kernels  84.4 us (97%)
  between operations  2.1 us (2%)
    pallas_call x1, Pallas kernels, body(): pl.pallas_call(kernel, out_shape=(pltpu.VMEM((8, 128), jnp.float32), pltp...  81.2 us
    pallas_call x1, Pallas kernels, body(): pl.pallas_call(functools.partial(finish, images), out_shape=(jax.ShapeDty...  3.23 us

profile of v6, /device:TPU:1, one launch (start us, length us, event | category | flops | bytes accessed | tf_op | source)
XLA Modules:
  0.0 86.6 jit_solution(16637701418294364014)
XLA Ops:
  1.9 0.1 iota.7.scalars
  2.0 81.2 %exchange.1 = (f32[8,128]{1,0:T(8,128)S(1)}, f32[2,512,1152]{2,1,0:T(8,128)S(1)}, bf16[2,512,1152]{2,1,0:T(8,128)(2,1)S(1)}, f32[2,512,128]{2,1,0:T(8,128)S(1)}) custom-call(bf16[512,1152]{1,0:T(8,128)(2,1)} %image.1, bf16[512,1152]{1,0:T(8,128)(2,1)} %text.1, s32[1,512]{1,0:T(1,128)} %bitcast.5, f32[8,128]{1,0:T(8,128)S(1)} %iota.7.scalars), custom_call_target="tpu_custom_call" | custom-call | flops 12683575296 | bytes 2359296 | tf_op jit(solution)/shard_map/exchange/pallas_call | solution.py:421
  83.2 3.2 %finish.1 = (f32[1]{0:T(128)}, f32[512,1152]{1,0:T(8,128)}, f32[512,1152]{1,0:T(8,128)}) custom-call(f32[8,128]{1,0:T(8,128)S(1)} %iota.7.scalars, f32[8,128]{1,0:T(8,128)S(1)} %get-tuple-element.7.total, f32[2,512,1152]{2,1,0:T(8,128)S(1)} %get-tuple-element.8.d, bf16[2,512,1152]{2,1,0:T(8,128)(2,1)S(1)} %get-tuple-element.9.raw, ...), custom_call_target="tpu_custom_call" | custom-call | flops 8257536 | bytes 4718592 | tf_op jit(solution)/shard_map/finish/pallas_call | solution.py:452
  (1 shorter events, 0.0 us)
